TPU v7x, 32 devices: a whole 2x2x4 slice. The times are simulated.
32 devices in a mesh: groups: 2 (over y), seq: 16 (over z, x, core).
Axes of the slice: x: 2, y: 2, z: 4, core: 2. Of those that a mesh axis runs over, the one named last changes fastest.
Arguments:
- queries: bfloat16 [8192, 2048], P(('groups', 'seq')), parts along dimension 0, may hold values from -6 to 6
- key_inputs: bfloat16 [8192, 2048], P(('groups', 'seq')), parts along dimension 0, may hold values from -6 to 6
- values: bfloat16 [8192, 2048], P(('groups', 'seq')), parts along dimension 0, may hold values from -6 to 6
- short_taps: float32 [3, 3, 2048], replicated, may hold values from -3.6 to 3.6
- decay_rates: float32 [2, 2048], replicated, may hold values from 2.4414063e-05 to 0.05, as said below
- residues: float32 [2, 2048], replicated, may hold values from -6 to 6
- skip_gain: float32 [2048], replicated, may hold values from -6 to 6
- out_weight: bfloat16 [2048, 4096], P('seq'), may hold values from -0.125 to 0.125
- cotangent: bfloat16 [8192, 4096], P(('groups', 'seq')), parts along dimension 0, may hold values from -6 to 6
- doc_blocks: int32 [8], P('groups'), parts along dimension 0, may hold values from 1 to 16, 32 in all
Outputs:
- mixed_out: bfloat16 [8192, 4096], P(('groups', 'seq')), parts along dimension 0
- grad_queries: bfloat16 [8192, 2048], P(('groups', 'seq')), parts along dimension 0
- grad_keys: bfloat16 [8192, 2048], P(('groups', 'seq')), parts along dimension 0
- grad_values: bfloat16 [8192, 2048], P(('groups', 'seq')), parts along dimension 0
There are 2 independent parts, one for each index of `groups`. A program takes and returns all parts, laid end to end along the dimension named above; an argument that names none is the same for every part. Nothing has to cross between parts.
Inputs may be any that keep to these rules, and one draw needn't show every extreme that they name: `doc_blocks`: documents fill the batch in order: the entries sum to 32, and the longest is exactly 16 blocks. `decay_rates`: positive decay rates.
All inputs are finite; a program needn't handle non-finite values.
Results may differ from a plain program's by a relative error of at most 0.0051.
Values may be sent and summed in bfloat16 or wider, within the bound.
A program may use at most 128 MiB of HBM per device.

v0:
```python
import jax
import jax.numpy as jnp
from jax import lax
from jax.sharding import PartitionSpec as P

BLOCK = 128
exact_mode = lax.Precision.HIGHEST


def from_behind(value, axis, steps):
    count = lax.axis_size(axis)
    leading, last = (max(0, -steps), min(count, count - steps))
    return lax.ppermute(value, axis, [(source, source + steps) for source in range(leading, last)])


def combine(earlier, later):
    return (earlier[0] * later[0], later[0] * earlier[1] + later[1])


def block_marks(doc_blocks, first_block, block_count):
    doc_ends = jnp.cumsum(doc_blocks)
    starts = doc_ends - doc_blocks
    block_index = first_block + jnp.arange(block_count, dtype=jnp.int32)
    matches = (block_index[:, None] == starts[None, :]) | (block_index[:, None] >= doc_ends[-1])
    return jnp.any(matches, axis=1).astype(jnp.float32)


def block_parts(blocked, decay_rates, reset_flags):
    span = blocked.shape[-1]
    offsets = jnp.arange(span, dtype=jnp.float32)
    upper_ones = (offsets[:, None] <= offsets[None, :]).astype(jnp.float32)
    growth = jnp.exp(decay_rates[:, :, None] * offsets[None, None, :])
    shrink = jnp.exp(-decay_rates[:, :, None] * offsets[None, None, :])
    lifted = blocked[None, :, :, :] * growth[:, :, None, :]
    inside = (
        jnp.einsum("sgbp,pt->sgbt", lifted, upper_ones, precision=exact_mode)
        * shrink[:, :, None, :]
    )
    keep_rate = (1.0 - reset_flags)[None, None, :] * jnp.exp(-decay_rates * span)[:, :, None]
    cum_keep, cum_ends = lax.associative_scan(combine, (keep_rate, inside[..., -1]), axis=2)
    return (inside, cum_keep, cum_ends)


def block_finish(inside, cum_keep, cum_ends, decay_rates, filter_weight, reset_flags, incoming):
    span = inside.shape[-1]
    at_end = cum_keep * incoming[:, :, None] + cum_ends
    before = (
        jnp.concatenate([incoming[:, :, None], at_end[:, :, :-1]], axis=2)
        * (1.0 - reset_flags)[None, None, :]
    )
    offsets = jnp.arange(1, span + 1, dtype=jnp.float32)
    decay_rows = jnp.exp(-decay_rates[:, :, None] * offsets[None, None, :])
    summed_up = inside + before[..., None] * decay_rows[:, :, None, :]
    return jnp.sum(summed_up * filter_weight[:, :, None, None], axis=0)


def relay_pass(columns, decay_rates, filter_weight, doc_blocks, backward):
    device_place = lax.axis_index("seq")
    spread = lax.all_to_all(columns, "seq", split_axis=0, concat_axis=1, tiled=True)
    share_width = spread.shape[0]
    block_count = spread.shape[1] // BLOCK
    own_rates = lax.dynamic_slice_in_dim(decay_rates, device_place * share_width, share_width, 1)
    own_weights = lax.dynamic_slice_in_dim(
        filter_weight, device_place * share_width, share_width, 1
    )
    lead_shift = 1 if backward else 0
    reset_flags = block_marks(doc_blocks, lead_shift, block_count)
    blocked = spread.reshape(share_width, block_count, BLOCK)
    if backward:
        blocked = jnp.flip(blocked, axis=(1, 2))
        reset_flags = jnp.flip(reset_flags, axis=0)
    inside, cum_keep, cum_ends = block_parts(blocked, own_rates, reset_flags)
    zero_state = jnp.zeros(own_rates.shape, jnp.float32)
    result = block_finish(
        inside, cum_keep, cum_ends, own_rates, own_weights, reset_flags, zero_state
    )
    if backward:
        result = jnp.flip(result, axis=(1, 2))
    return lax.all_to_all(
        result.reshape(share_width, block_count * BLOCK),
        "seq",
        split_axis=1,
        concat_axis=0,
        tiled=True,
    )


def long_conv(columns, decay_rates, filter_weight, doc_blocks, backward):
    return relay_pass(columns, decay_rates, filter_weight, doc_blocks, backward)


def on_device(
    queries,
    key_inputs,
    values,
    short_taps,
    decay_rates,
    residues,
    skip_gain,
    out_weight,
    cotangent,
    doc_blocks,
):
    row_count = queries.shape[0]
    block_count = row_count // BLOCK
    marks_ext = block_marks(doc_blocks, lax.axis_index("seq") * block_count, block_count + 1)
    head_mask = (jnp.arange(BLOCK) == 0).astype(jnp.float32)
    begins = (marks_ext[:, None] * head_mask[None, :]).reshape(-1)[: row_count + 2]
    now_start = begins[:row_count]
    prior_start = jnp.concatenate([jnp.zeros((1,), jnp.float32), now_start[:-1]])
    keep_one = (1.0 - now_start)[:, None]
    keep_two = keep_one * (1.0 - prior_start)[:, None]
    next_one = (1.0 - begins[1 : row_count + 1])[:, None]
    next_two = next_one * (1.0 - begins[2 : row_count + 2])[:, None]
    tail_rows = jnp.stack(
        [queries[row_count - 2 :], key_inputs[row_count - 2 :], values[row_count - 2 :]]
    )
    prev_rims = from_behind(tail_rows, "seq", 1)

    def forward_short(current, rim_rows, tap_row):
        longer = jnp.concatenate([rim_rows, current], axis=0).astype(jnp.float32)
        return (
            tap_row[0] * longer[2:]
            + tap_row[1] * keep_one * longer[1:-1]
            + tap_row[2] * keep_two * longer[:-2]
        )

    q_short = forward_short(queries, prev_rims[0], short_taps[0])
    k_short = forward_short(key_inputs, prev_rims[1], short_taps[1])
    v_short = forward_short(values, prev_rims[2], short_taps[2])
    product = k_short * v_short
    filter_weight = residues * jnp.sqrt(2.0 * decay_rates)
    conv_out = (
        long_conv(product.T, decay_rates, filter_weight, doc_blocks, False).T + skip_gain * product
    )
    gated_rows = (q_short * conv_out).astype(jnp.bfloat16)
    weight_piece = lax.all_gather(out_weight, "seq", axis=0, tiled=True)
    total_out = jnp.dot(gated_rows, weight_piece, preferred_element_type=jnp.float32)
    column = lax.dot_general(
        cotangent, weight_piece, (((1,), (1,)), ((), ())), preferred_element_type=jnp.float32
    )
    total_out, grad_gated = (total_out, column)
    mixed_out = total_out.astype(jnp.bfloat16)
    grad_qs = grad_gated * conv_out
    grad_conv = grad_gated * q_short
    grad_product = (
        long_conv(grad_conv.T, decay_rates, filter_weight, doc_blocks, True).T
        + skip_gain * grad_conv
    )
    grad_ks = grad_product * v_short
    grad_vs = grad_product * k_short
    head_rows = jnp.stack([grad_qs[:2], grad_ks[:2], grad_vs[:2]])
    next_rims = from_behind(head_rows.astype(jnp.bfloat16), "seq", -1).astype(head_rows.dtype)

    def backward_short(gradient, rim_rows, tap_row):
        longer = jnp.concatenate([gradient, rim_rows], axis=0)
        summed = (
            tap_row[0] * gradient
            + tap_row[1] * next_one * longer[1 : row_count + 1]
            + tap_row[2] * next_two * longer[2:]
        )
        return summed.astype(jnp.bfloat16)

    grad_queries = backward_short(grad_qs, next_rims[0], short_taps[0])
    grad_keys = backward_short(grad_ks, next_rims[1], short_taps[1])
    grad_values = backward_short(grad_vs, next_rims[2], short_taps[2])
    return (mixed_out, grad_queries, grad_keys, grad_values)


def solution(mesh):
    return jax.shard_map(
        on_device,
        mesh=mesh,
        in_specs=(
            P(("groups", "seq"), None),
            P(("groups", "seq"), None),
            P(("groups", "seq"), None),
            P(),
            P(),
            P(),
            P(),
            P("seq", None),
            P(("groups", "seq"), None),
            P("groups"),
        ),
        out_specs=(
            P(("groups", "seq"), None),
            P(("groups", "seq"), None),
            P(("groups", "seq"), None),
            P(("groups", "seq"), None),
        ),
        check_vma=False,
    )
```

profile of v0, /device:TPU:16, one launch (start us, length us, event | category | flops | bytes accessed | tf_op | source)
XLA Modules:
  0.0 414.4 jit_solution(16186817507365080882)
XLA Ops:
  7.2 0.7 all-gather.2.cloned.1.call-update
  7.9 0.8 slice_bitcast_fusion.8
  8.7 0.8 slice_bitcast_fusion.6
  9.6 1.9 collective-permute-start
  11.5 0.8 reduce-window.4
  12.9 0.7 broadcast_compare_fusion.1
  13.6 0.7 bitcast_subtract_fusion
  14.5 0.7 fusion.63
  15.2 1.6 fusion.71
  16.9 0.6 slice_bitcast_fusion.4
  18.2 3.1 multiply_bitcast_fusion.1
  21.4 1.5 copy.42
  22.9 6.6 %all-to-all-start = ((f32[16,128,256]{1,2,0:T(8,128)}), f32[16,128,256]{1,2,0:T(8,128)}, u32[]{:S(2)}, u32[]{:S(2)}) async-start(f32[16,128,256]{1,2,0:T(8,128)} %bitcast.121), calls=%async_computation | async-start | bytes 4194304 | tf_op jit(solution)/shard_map/all_to_all | solution.py:59
  29.5 0.7 iota_compare_fusion.2
  30.3 1.3 dynamic-slice_multiply_fusion
  32.9 0.6 slice.510
  33.5 0.6 slice.491
  34.1 0.6 slice.490
  35.3 0.6 slice.558
  35.9 0.6 slice.539
  36.5 0.6 slice.538
  37.2 0.8 multiply_exponential_fusion
  38.0 2.5 maximum_convert_fusion
  40.5 68.7 %all-to-all-done = f32[16,128,256]{1,2,0:T(8,128)} async-done(((f32[16,128,256]{1,2,0:T(8,128)}), f32[16,128,256]{1,2,0:T(8,128)}, u32[]{:S(2)}, u32[]{:S(2)}) %all-to-all-start) | async-done | bytes 2097184 | tf_op jit(solution)/shard_map/all_to_all | solution.py:59
  109.2 2.9 copy.23
  112.2 60.0 %all-gather.2.cloned.1.call-done = bf16[2048,4096]{1,0:T(8,128)(2,1)} async-done(((bf16[128,4096]{1,0:T(8,128)(2,1)}), bf16[2048,4096]{1,0:T(8,128)(2,1)}) %all-gather.2.cloned.1.call-update) | async-done | bytes 16777232 | tf_op jit(solution)/shard_map/all_gather | solution.py:137
  172.2 9.5 %fusion.82 = f32[256,2048]{1,0:T(8,128)} fusion(bf16[256,4096]{1,0:T(8,128)(2,1)S(1)} %copy-done, bf16[2048,4096]{1,0:T(8,128)(2,1)} %all-gather.2.cloned.1.call-done), kind=kOutput, calls=%fused_computation.202 | convolution fusion | flops 4294967296 | bytes 20971520 | tf_op jit(solution)/shard_map/dot_general | solution.py:139
  181.7 6.8 %multiply_bitcast_fusion = (f32[32,16,8,128]{3,2,1,0:T(8,128)S(1)}, f32[256,2048]{1,0:T(8,128)}) fusion(f32[256,2048]{1,0:T(8,128)} %fusion.82, f32[258,2048]{1,0:T(8,128)} %maximum_convert_fusion, f32[256]{0:T(256)S(1)} %copy-done.30, f32[2048]{0:T(1024)S(1)} %bitcast.143, f32[256]{0:T(256)S(1)} %copy-done.28, f32[2048]{0:T(1024)S(1)} %bitcast.145, ...), kind=kLoop, calls=%fused_computation.65 | loop fusion | flops 4194304 | bytes 12609536
  188.4 1.5 copy.41
  190.0 6.7 %all-to-all-start.2 = ((f32[16,128,256]{1,2,0:T(8,128)}), f32[16,128,256]{1,2,0:T(8,128)}, u32[]{:S(2)}, u32[]{:S(2)}) async-start(f32[16,128,256]{1,2,0:T(8,128)} %bitcast.120), calls=%async_computation.2 | async-start | bytes 4194304 | tf_op jit(solution)/shard_map/all_to_all | solution.py:59
  196.7 2.8 fusion.4
  199.6 2.0 copy-done.4
  202.9 41.5 %all-to-all-done.2 = f32[16,128,256]{1,2,0:T(8,128)} async-done(((f32[16,128,256]{1,2,0:T(8,128)}), f32[16,128,256]{1,2,0:T(8,128)}, u32[]{:S(2)}, u32[]{:S(2)}) %all-to-all-start.2) | async-done | bytes 2097184 | tf_op jit(solution)/shard_map/all_to_all | solution.py:59
  244.4 16.5 %rev.11 = f32[128,32,128]{0,2,1:T(8,128)} reverse(f32[128,32,128]{0,2,1:T(8,128)} %bitcast.32), dimensions={1,2} | reverse | bytes 4194304 | tf_op jit(solution)/shard_map/jit(_flip)/rev | solution.py:70
  260.9 1.9 copy.27
  262.9 2.8 fusion.7
  265.8 2.0 copy-done.5
  269.1 6.8 %multiply_reduce_fusion = (f32[128,32,128]{0,2,1:T(8,128)S(1)}, f32[128,32,128]{0,2,1:T(8,128)}) fusion(f32[2,128,32,128]{1,3,2,0:T(8,128)} %copy-done.5, f32[2,128,32]{1,2,0:T(8,128)S(1)} %pad_multiply_fusion, f32[2,128]{1,0:T(2,128)S(1)} %copy-done.33, f32[2,128,128]{1,2,0:T(8,128)S(1)} %get-tuple-element.90, f32[2,128,32,128]{1,3,2,0:T(8,128)} %copy-done.4, ...), kind=kLoop, calls=%fused_computation.1 | loop fusion | flops 7340032 | bytes 12780544 | tf_op jit(solution)/shard_map/reduce_sum | solution.py:54
  275.9 4.7 %all-to-all-start.1 = ((f32[128,16,256]{0,2,1:T(8,128)}), f32[128,16,256]{0,2,1:T(8,128)}, u32[]{:S(2)}, u32[]{:S(2)}) async-start(f32[128,16,256]{0,2,1:T(8,128)} %bitcast.119), calls=%async_computation.1 | async-start | bytes 4194304 | tf_op jit(solution)/shard_map/all_to_all | solution.py:79
  280.6 10.3 %rev.13 = f32[128,32,128]{0,2,1:T(8,128)} reverse(f32[128,32,128]{0,2,1:T(8,128)S(1)} %get-tuple-element.4), dimensions={1,2} | reverse | bytes 4194304 | tf_op jit(solution)/shard_map/jit(_flip)/rev | solution.py:78
  290.9 37.5 %all-to-all-done.1 = f32[128,16,256]{0,2,1:T(8,128)} async-done(((f32[128,16,256]{0,2,1:T(8,128)}), f32[128,16,256]{0,2,1:T(8,128)}, u32[]{:S(2)}, u32[]{:S(2)}) %all-to-all-start.1) | async-done | bytes 2097184 | tf_op jit(solution)/shard_map/all_to_all | solution.py:79
  328.4 4.8 %all-to-all-start.3 = ((f32[128,16,256]{0,2,1:T(8,128)}), f32[128,16,256]{0,2,1:T(8,128)}, u32[]{:S(2)}, u32[]{:S(2)}) async-start(f32[128,16,256]{0,2,1:T(8,128)} %bitcast.122), calls=%async_computation.3 | async-start | bytes 4194304 | tf_op jit(solution)/shard_map/all_to_all | solution.py:79
  333.3 47.7 %all-to-all-done.3 = f32[128,16,256]{0,2,1:T(8,128)} async-done(((f32[128,16,256]{0,2,1:T(8,128)}), f32[128,16,256]{0,2,1:T(8,128)}, u32[]{:S(2)}, u32[]{:S(2)}) %all-to-all-start.3) | async-done | bytes 2097184 | tf_op jit(solution)/shard_map/all_to_all | solution.py:79
  380.9 5.2 %fusion.64 = (f32[256,2048]{1,0:T(8,128)S(1)}, f32[256,2048]{1,0:T(8,128)S(1)}, f32[256,2048]{1,0:T(8,128)S(1)}, f32[256,2048]{1,0:T(8,128)S(1)}) fusion(f32[256,2048]{1,0:T(8,128)} %get-tuple-element.13, f32[256,2048]{1,0:T(8,128)} %fusion.82, f32[256,2048]{1,0:T(8,128)} %get-tuple-element.18, f32[2048]{0:T(1024)S(1)} %copy-done.31, ...), kind=kLoop, calls=%fused_computation.189 | loop fusion | flops 4194304 | bytes 20979712 | tf_op jit(solution)/shard_map/mul | solution.py:150
  386.6 3.2 collective-permute-start.1
  389.8 11.6 %convolution_convert_fusion = bf16[256,4096]{1,0:T(8,128)(2,1)} fusion(bf16[2048,4096]{1,0:T(8,128)(2,1)} %all-gather.2.cloned.1.call-done, f32[256,2048]{1,0:T(8,128)S(1)} %copy-done.6, f32[256,2048]{1,0:T(8,128)S(1)} %get-tuple-element.20), kind=kOutput, calls=%fused_computation | convolution fusion | flops 4297064448 | bytes 23068672 | tf_op jit(solution)/shard_map/dot_general | solution.py:138
  401.5 1.9 fusion.24
  403.4 4.2 %fusion.14 = (bf16[256,2048]{1,0:T(8,128)(2,1)}, bf16[256,2048]{1,0:T(8,128)(2,1)}) fusion(f32[256,2048]{1,0:T(8,128)S(1)} %mul.732, f32[2,2048]{1,0:T(2,128)S(1)} %get-tuple-element.30, f32[256]{0:T(256)S(1)} %get-tuple-element.71, f32[256]{0:T(256)S(1)} %get-tuple-element.70, f32[2048]{0:T(1024)S(1)} %bitcast.140, f32[2048]{0:T(1024)S(1)} %bitcast.142, ...), kind=kLoop, calls=%fused_computation.19 | loop fusion | flops 10485760 | bytes 6375424 | tf_op jit(solution)/shard_map/convert_element_type | solution.py:162
  (247 shorter events, 6.3 us)
Async XLA Ops:
  7.2 165.0 %copy-start = (bf16[256,4096]{1,0:T(8,128)(2,1)S(1)}, bf16[256,4096]{1,0:T(8,128)(2,1)}, u32[]{:S(2)}) copy-start(bf16[256,4096]{1,0:T(8,128)(2,1)} %param.18) | copy-start | bytes 6291460
  7.2 10.4 %copy-start.7 = (bf16[256,2048]{1,0:T(8,128)(2,1)S(1)}, bf16[256,2048]{1,0:T(8,128)(2,1)}, u32[]{:S(2)}) copy-start(bf16[256,2048]{1,0:T(8,128)(2,1)} %param.11) | copy-start | bytes 3145732
  7.2 165.0 %all-gather.2.cloned.1.call-start = ((), (), s32[]{:S(2)}) async-start(), calls=%async_computation.4 | async-start | bytes 17825792 | tf_op jit(solution)/shard_map/all_gather | solution.py:137
  9.6 7.4 %collective-permute-start = (bf16[3,2,2048]{2,1,0:T(2,128)(2,1)S(1)}, bf16[3,2,2048]{2,1,0:T(2,128)(2,1)S(1)}, u32[]{:S(2)}, u32[]{:S(2)}) collective-permute-start(bf16[3,2,2048]{2,1,0:T(2,128)(2,1)S(1)} %pad_maximum_fusion.3), channel_id=1, source_target_pairs={{0,1},{1,2},{2,3},{3,4},{4,5},{5,6},{6,7},{7,8},{8,9},{9,10},{10,1... | collective-permute-start | bytes 73736 | tf_op jit(solution)/shard_map/ppermute | solution.py:13
  12.9 4.9 %copy-start.8 = (bf16[256,2048]{1,0:T(8,128)(2,1)S(1)}, bf16[256,2048]{1,0:T(8,128)(2,1)}, u32[]{:S(2)}) copy-start(bf16[256,2048]{1,0:T(8,128)(2,1)} %param.12) | copy-start | bytes 3145732
  16.8 1.4 copy-start.10
  16.8 1.4 copy-start.12
  16.8 1.4 copy-start.14
  16.8 1.4 copy-start.16
  16.9 1.3 copy-start.27
  16.9 1.3 copy-start.29
  22.9 15.1 %copy-start.9 = (bf16[256,2048]{1,0:T(8,128)(2,1)S(1)}, bf16[256,2048]{1,0:T(8,128)(2,1)}, u32[]{:S(2)}) copy-start(bf16[256,2048]{1,0:T(8,128)(2,1)} %param.10) | copy-start | bytes 3145732
  22.9 86.3 %all-to-all-start = ((f32[16,128,256]{1,2,0:T(8,128)}), f32[16,128,256]{1,2,0:T(8,128)}, u32[]{:S(2)}, u32[]{:S(2)}) async-start(f32[16,128,256]{1,2,0:T(8,128)} %bitcast.121), calls=%async_computation | async-start | bytes 4194304 | tf_op jit(solution)/shard_map/all_to_all | solution.py:59
  31.6 5.5 %copy-start.36 = (f32[32]{0:T(128)}, f32[32]{0:T(128)S(1)}, u32[]{:S(2)}) copy-start(f32[32]{0:T(128)S(1)} %broadcast_subtract_fusion.1) | copy-start | bytes 388
  31.6 5.5 %copy-start.38 = (f32[32]{0:T(128)}, f32[32]{0:T(128)S(1)}, u32[]{:S(2)}) copy-start(f32[32]{0:T(128)S(1)} %convert_subtract_fusion) | copy-start | bytes 388
  112.1 69.5 %copy-start.18 = (f32[1,1,2048]{2,1,0:T(1,128)S(1)}, f32[1,1,2048]{2,1,0:T(1,128)}, u32[]{:S(2)}) copy-start(f32[1,1,2048]{2,1,0:T(1,128)} %get-tuple-element.25) | copy-start | bytes 24580
  112.1 69.5 %copy-start.19 = (f32[1,1,2048]{2,1,0:T(1,128)S(1)}, f32[1,1,2048]{2,1,0:T(1,128)}, u32[]{:S(2)}) copy-start(f32[1,1,2048]{2,1,0:T(1,128)} %get-tuple-element.26) | copy-start | bytes 24580
  112.1 69.5 %copy-start.20 = (f32[1,1,2048]{2,1,0:T(1,128)S(1)}, f32[1,1,2048]{2,1,0:T(1,128)}, u32[]{:S(2)}) copy-start(f32[1,1,2048]{2,1,0:T(1,128)} %get-tuple-element.27) | copy-start | bytes 24580
  112.1 69.5 %copy-start.28 = (f32[256]{0:T(256)S(1)}, f32[256]{0:T(256)}, u32[]{:S(2)}) copy-start(f32[256]{0:T(256)} %copy-done.27) | copy-start | bytes 3076
  112.1 69.5 %copy-start.30 = (f32[256]{0:T(256)S(1)}, f32[256]{0:T(256)}, u32[]{:S(2)}) copy-start(f32[256]{0:T(256)} %copy-done.29) | copy-start | bytes 3076
  190.0 6.7 %copy-start.2 = (f32[128,32,128]{2,0,1:T(8,128)S(1)}, f32[128,32,128]{2,0,1:T(8,128)}, u32[]{:S(2)}) copy-start(f32[128,32,128]{2,0,1:T(8,128)} %copy.23) | copy-start | bytes 6291460
  190.0 54.5 %all-to-all-start.2 = ((f32[16,128,256]{1,2,0:T(8,128)}), f32[16,128,256]{1,2,0:T(8,128)}, u32[]{:S(2)}, u32[]{:S(2)}) async-start(f32[16,128,256]{1,2,0:T(8,128)} %bitcast.120), calls=%async_computation.2 | async-start | bytes 4194304 | tf_op jit(solution)/shard_map/all_to_all | solution.py:59
  196.7 5.0 %copy-start.23 = (f32[2,128,16]{1,2,0:T(8,128)S(1)}, f32[2,128,16]{1,2,0:T(8,128)}, u32[]{:S(2)}) copy-start(f32[2,128,16]{1,2,0:T(8,128)} %slice.491) | copy-start | bytes 49156
  196.7 5.0 %copy-start.24 = (f32[2,128,16]{1,2,0:T(8,128)S(1)}, f32[2,128,16]{1,2,0:T(8,128)}, u32[]{:S(2)}) copy-start(f32[2,128,16]{1,2,0:T(8,128)} %slice.490) | copy-start | bytes 49156
  196.7 6.0 %copy-start.26 = (f32[2,128,15]{1,2,0:T(8,128)S(1)}, f32[2,128,15]{1,2,0:T(8,128)}, u32[]{:S(2)}) copy-start(f32[2,128,15]{1,2,0:T(8,128)} %slice.510) | copy-start | bytes 46084
  196.7 6.0 %copy-start.35 = (f32[2,128,1]{1,2,0:T(1,128)S(1)}, f32[2,128,1]{1,2,0:T(1,128)}, u32[]{:S(2)}) copy-start(f32[2,128,1]{1,2,0:T(1,128)} %slice.607) | copy-start | bytes 3076
  196.7 6.2 %copy-start.39 = (f32[32]{0:T(128)S(1)}, f32[32]{0:T(128)}, u32[]{:S(2)}) copy-start(f32[32]{0:T(128)} %copy-done.38) | copy-start | bytes 388
  199.5 2.1 copy-start.4
  262.9 5.0 %copy-start.21 = (f32[2,128,16]{1,2,0:T(8,128)S(1)}, f32[2,128,16]{1,2,0:T(8,128)}, u32[]{:S(2)}) copy-start(f32[2,128,16]{1,2,0:T(8,128)} %slice.539) | copy-start | bytes 49156
  262.9 5.0 %copy-start.22 = (f32[2,128,16]{1,2,0:T(8,128)S(1)}, f32[2,128,16]{1,2,0:T(8,128)}, u32[]{:S(2)}) copy-start(f32[2,128,16]{1,2,0:T(8,128)} %slice.538) | copy-start | bytes 49156
  262.9 6.0 %copy-start.25 = (f32[2,128,15]{1,2,0:T(8,128)S(1)}, f32[2,128,15]{1,2,0:T(8,128)}, u32[]{:S(2)}) copy-start(f32[2,128,15]{1,2,0:T(8,128)} %slice.558) | copy-start | bytes 46084
  262.9 6.0 %copy-start.34 = (f32[2,128,1]{1,2,0:T(1,128)S(1)}, f32[2,128,1]{1,2,0:T(1,128)}, u32[]{:S(2)}) copy-start(f32[2,128,1]{1,2,0:T(1,128)} %slice.639) | copy-start | bytes 3076
  262.9 6.1 %copy-start.37 = (f32[32]{0:T(128)S(1)}, f32[32]{0:T(128)}, u32[]{:S(2)}) copy-start(f32[32]{0:T(128)} %copy-done.36) | copy-start | bytes 388
  262.9 6.2 %copy-start.33 = (f32[2,128]{1,0:T(2,128)S(1)}, f32[2,128]{1,0:T(2,128)}, u32[]{:S(2)}) copy-start(f32[2,128]{1,0:T(2,128)} %get-tuple-element.15) | copy-start | bytes 3076
  265.8 2.0 copy-start.5
  275.9 52.4 %all-to-all-start.1 = ((f32[128,16,256]{0,2,1:T(8,128)}), f32[128,16,256]{0,2,1:T(8,128)}, u32[]{:S(2)}, u32[]{:S(2)}) async-start(f32[128,16,256]{0,2,1:T(8,128)} %bitcast.119), calls=%async_computation.1 | async-start | bytes 4194304 | tf_op jit(solution)/shard_map/all_to_all | solution.py:79
  328.4 4.8 %copy-start.32 = (f32[384]{0:T(512)S(1)}, f32[384]{0:T(512)}, u32[]{:S(2)}) copy-start(f32[384]{0:T(512)} %get-tuple-element.86) | copy-start | bytes 4612
  328.4 52.6 %copy-start.3 = (f32[256,2048]{1,0:T(8,128)S(1)}, f32[256,2048]{1,0:T(8,128)}, u32[]{:S(2)}) copy-start(f32[256,2048]{1,0:T(8,128)} %get-tuple-element.14) | copy-start | bytes 6291460
  328.4 52.6 %copy-start.31 = (f32[2048]{0:T(1024)S(1)}, f32[2048]{0:T(1024)}, u32[]{:S(2)}) copy-start(f32[2048]{0:T(1024)} %param.16) | copy-start | bytes 24580
  328.4 52.6 %all-to-all-start.3 = ((f32[128,16,256]{0,2,1:T(8,128)}), f32[128,16,256]{0,2,1:T(8,128)}, u32[]{:S(2)}, u32[]{:S(2)}) async-start(f32[128,16,256]{0,2,1:T(8,128)} %bitcast.122), calls=%async_computation.3 | async-start | bytes 4194304 | tf_op jit(solution)/shard_map/all_to_all | solution.py:79
  386.2 3.6 copy-start.6
  386.6 14.8 %collective-permute-start.1 = (bf16[3,2,2048]{2,1,0:T(2,128)(2,1)S(1)}, bf16[3,2,2048]{2,1,0:T(2,128)(2,1)S(1)}, u32[]{:S(2)}, u32[]{:S(2)}) collective-permute-start(bf16[3,2,2048]{2,1,0:T(2,128)(2,1)S(1)} %pad_maximum_fusion.4), channel_id=1, source_target_pairs={{1,0},{2,1},{3,2},{4,3},{5,4},{6,5},{7,6},{8,7},{9,8},{10,9},{11,1... | collective-permute-start | bytes 73736 | tf_op jit(solution)/shard_map/ppermute | solution.py:13
  401.4 2.0 copy-start.11
  401.4 2.0 copy-start.13
  401.4 2.0 copy-start.15
  401.4 2.0 copy-start.17
  403.4 4.2 %copy-start.1 = (bf16[256,4096]{1,0:T(8,128)(2,1)S(1)}, bf16[256,4096]{1,0:T(8,128)(2,1)}, u32[]{:S(2)}) copy-start(bf16[256,4096]{1,0:T(8,128)(2,1)} %param.18) | copy-start | bytes 6291460
Sparse Core Ops, SparseCore 0:
  10.2 161.9 all-gather.1
where the time goes:
time: 416 us; the launch traced here: 414 us
  waiting for transfers between devices  256 us (62%)
  local copies, waits for them, and re-layouts  49.7 us (12%)
  other arithmetic  38.9 us (9%)
  starting transfers between devices  28 us (7%)
  matrix products  26.6 us (6%)
  between operations  15.2 us (4%)
    all_to_all x2, waiting for transfers between devices, relay_pass(): lax.all_to_all(columns, 'seq', split_axis=0, concat_axis=1, tiled=True)  110 us
    all_to_all x2, waiting for transfers between devices, relay_pass(): lax.all_to_all(result.reshape(share_width, block_count * BLOCK), 'seq', s...  85.2 us
    all_gather x1, waiting for transfers between devices, on_device(): weight_piece = lax.all_gather(out_weight, 'seq', axis=0, tiled=True)  60 us
    rev x2, local copies, waits for them, and re-layouts, relay_pass(): blocked = jnp.flip(blocked, axis=(1, 2))  18.5 us
    all_to_all x2, starting transfers between devices, relay_pass(): lax.all_to_all(columns, 'seq', split_axis=0, concat_axis=1, tiled=True)  13.3 us
    dot_general x1, matrix products, on_device(): jnp.dot(gated_rows, weight_piece, preferred_element_type=jnp.float32)  11.6 us
    rev x1, local copies, waits for them, and re-layouts, relay_pass(): result = jnp.flip(result, axis=(1, 2))  10.3 us
    unnamed x2, other arithmetic  9.89 us
  transfers between devices with their start and end apart: 7, of which 5 were waited for; matrix products, arithmetic and copies ran while one was open for 13% of the time, Pallas kernels for 0%

commit v1 on v0

--- a/solution.py
+++ b/solution.py
@@ -5,6 +5,19 @@
 
 BLOCK = 128
 exact_mode = lax.Precision.HIGHEST
+
+
+def gather_around(x, axis, dim):
+    size, index, extent = (lax.axis_size(axis), lax.axis_index(axis), x.shape[dim])
+    forward = [(i, (i + 1) % size) for i in range(size)]
+    result = jnp.zeros((*x.shape[:dim], size * extent, *x.shape[dim + 1 :]), x.dtype)
+    held = x
+    for step in range(size):
+        owner = (index - step) % size
+        result = lax.dynamic_update_slice_in_dim(result, held, owner * extent, axis=dim)
+        if step < size - 1:
+            held = lax.ppermute(held, axis, forward)
+    return result
 
 
 def from_behind(value, axis, steps):
@@ -134,7 +147,7 @@
         long_conv(product.T, decay_rates, filter_weight, doc_blocks, False).T + skip_gain * product
     )
     gated_rows = (q_short * conv_out).astype(jnp.bfloat16)
-    weight_piece = lax.all_gather(out_weight, "seq", axis=0, tiled=True)
+    weight_piece = gather_around(out_weight, "seq", 0)
     total_out = jnp.dot(gated_rows, weight_piece, preferred_element_type=jnp.float32)
     column = lax.dot_general(
         cotangent, weight_piece, (((1,), (1,)), ((), ())), preferred_element_type=jnp.float32

time: 416 us -> 518 us (1.25)
  waiting for transfers between devices: 256 us -> 328 us
  local copies, waits for them, and re-layouts: 49.7 us -> 84.4 us
  between operations: 15.2 us -> 2.18 us
  starting transfers between devices: 28 us -> 40.5 us
    ppermute x0 -> x15, waiting for transfers between devices: none -> 202 us  [gather_around(): held = lax.ppermute(held, axis, forward)]
    all_to_all x2, waiting for transfers between devices: 110 us -> 41.5 us  [relay_pass(): lax.all_to_all(columns, 'seq', split_axis=0, concat_axis=1, tiled=True)]
    all_gather x1 -> x0, waiting for transfers between devices: 60 us -> none  [on_device(): weight_piece = lax.all_gather(out_weight, 'seq', axis=0, tiled=True)]
    dynamic_update_slice x0 -> x16, local copies, waits for them, and re-layouts: none -> 27.1 us  [gather_around(): lax.dynamic_update_slice_in_dim(result, held, owner * extent, axis=dim)]
    all_to_all x2, starting transfers between devices: 13.3 us -> 25.5 us  [relay_pass(): lax.all_to_all(columns, 'seq', split_axis=0, concat_axis=1, tiled=True)]
    broadcast_in_dim x0 -> x1, local copies, waits for them, and re-layouts: none -> 6.02 us  [gather_around(): jnp.zeros((*x.shape[:dim], size * extent, *x.shape[dim + 1:]), x.dtype)]
  transfers between devices with their start and end apart: 7 -> 21, of which waited for: 5 -> 17; matrix products, arithmetic and copies ran while one was open for 13% -> 16% of each run, Pallas kernels for 0% -> 0%
where the time goes in v1:
time: 518 us; the launch traced here: 516 us
  waiting for transfers between devices  328 us (63%)
  local copies, waits for them, and re-layouts  84.4 us (16%)
  starting transfers between devices  40.5 us (8%)
  other arithmetic  34.8 us (7%)
  matrix products  25.5 us (5%)
    ppermute x15, waiting for transfers between devices, gather_around(): held = lax.ppermute(held, axis, forward)  202 us
    all_to_all x2, waiting for transfers between devices, relay_pass(): lax.all_to_all(result.reshape(share_width, block_count * BLOCK), 'seq', s...  85.3 us
    all_to_all x2, waiting for transfers between devices, relay_pass(): lax.all_to_all(columns, 'seq', split_axis=0, concat_axis=1, tiled=True)  41.5 us
    dynamic_update_slice x16, local copies, waits for them, and re-layouts, gather_around(): lax.dynamic_update_slice_in_dim(result, held, owner * extent, axis=dim)  27.1 us
    all_to_all x2, starting transfers between devices, relay_pass(): lax.all_to_all(columns, 'seq', split_axis=0, concat_axis=1, tiled=True)  25.5 us
    rev x2, local copies, waits for them, and re-layouts, relay_pass(): blocked = jnp.flip(blocked, axis=(1, 2))  18.4 us
    dot_general x1, matrix products, on_device(): jnp.dot(gated_rows, weight_piece, preferred_element_type=jnp.float32)  11.6 us
  transfers between devices with their start and end apart: 21, of which 17 were waited for; matrix products, arithmetic and copies ran while one was open for 16% of the time, Pallas kernels for 0%

profile of v1, /device:TPU:16, one launch (start us, length us, event | category | flops | bytes accessed | tf_op | source)
XLA Modules:
  0.0 515.7 jit_solution(15141145278257511311)
XLA Ops:
  0.7 15.3 %collective-permute-done.1 = bf16[128,4096]{1,0:T(8,128)(2,1)S(1)} collective-permute-done((bf16[128,4096]{1,0:T(8,128)(2,1)}, bf16[128,4096]{1,0:T(8,128)(2,1)S(1)}, u32[]{:S(2)}, u32[]{:S(2)}) %collective-permute-start.1) | collective-permute-done | bytes 1048608 | tf_op jit(solution)/shard_map/ppermute | solution.py:19
  17.0 14.2 %collective-permute-done.2 = bf16[128,4096]{1,0:T(8,128)(2,1)S(1)} collective-permute-done((bf16[128,4096]{1,0:T(8,128)(2,1)S(1)}, bf16[128,4096]{1,0:T(8,128)(2,1)S(1)}, u32[]{:S(2)}, u32[]{:S(2)}) %collective-permute-start.2) | collective-permute-done | bytes 1048608 | tf_op jit(solution)/shard_map/ppermute | solution.py:19
  31.2 15.1 %collective-permute-done.3 = bf16[128,4096]{1,0:T(8,128)(2,1)S(1)} collective-permute-done((bf16[128,4096]{1,0:T(8,128)(2,1)S(1)}, bf16[128,4096]{1,0:T(8,128)(2,1)S(1)}, u32[]{:S(2)}, u32[]{:S(2)}) %collective-permute-start.3) | collective-permute-done | bytes 1048608 | tf_op jit(solution)/shard_map/ppermute | solution.py:19
  47.3 15.2 %collective-permute-done.4 = bf16[128,4096]{1,0:T(8,128)(2,1)} collective-permute-done((bf16[128,4096]{1,0:T(8,128)(2,1)S(1)}, bf16[128,4096]{1,0:T(8,128)(2,1)}, u32[]{:S(2)}, u32[]{:S(2)}) %collective-permute-start.4) | collective-permute-done | bytes 1048608 | tf_op jit(solution)/shard_map/ppermute | solution.py:19
  64.1 1.9 collective-permute-start
  66.1 11.9 %collective-permute-done.5 = bf16[128,4096]{1,0:T(8,128)(2,1)} collective-permute-done((bf16[128,4096]{1,0:T(8,128)(2,1)}, bf16[128,4096]{1,0:T(8,128)(2,1)}, u32[]{:S(2)}, u32[]{:S(2)}) %collective-permute-start.5) | collective-permute-done | bytes 1048608 | tf_op jit(solution)/shard_map/ppermute | solution.py:19
  81.5 11.8 %collective-permute-done.6 = bf16[128,4096]{1,0:T(8,128)(2,1)} collective-permute-done((bf16[128,4096]{1,0:T(8,128)(2,1)}, bf16[128,4096]{1,0:T(8,128)(2,1)}, u32[]{:S(2)}, u32[]{:S(2)}) %collective-permute-start.6) | collective-permute-done | bytes 1048608 | tf_op jit(solution)/shard_map/ppermute | solution.py:19
  96.4 12.4 %collective-permute-done.7 = bf16[128,4096]{1,0:T(8,128)(2,1)} collective-permute-done((bf16[128,4096]{1,0:T(8,128)(2,1)}, bf16[128,4096]{1,0:T(8,128)(2,1)}, u32[]{:S(2)}, u32[]{:S(2)}) %collective-permute-start.7) | collective-permute-done | bytes 1048608 | tf_op jit(solution)/shard_map/ppermute | solution.py:19
  110.7 3.2 multiply_bitcast_fusion.1
  115.5 18.2 %all-to-all-start = ((f32[16,128,256]{1,2,0:T(8,128)}), f32[16,128,256]{1,2,0:T(8,128)}, u32[]{:S(2)}, u32[]{:S(2)}) async-start(f32[16,128,256]{1,2,0:T(8,128)} %bitcast.122), calls=%async_computation | async-start | bytes 4194304 | tf_op jit(solution)/shard_map/all_to_all | solution.py:72
  136.3 56.3 %collective-permute-done.9 = bf16[128,4096]{1,0:T(8,128)(2,1)S(1)} collective-permute-done((bf16[128,4096]{1,0:T(8,128)(2,1)}, bf16[128,4096]{1,0:T(8,128)(2,1)S(1)}, u32[]{:S(2)}, u32[]{:S(2)}) %collective-permute-start.9) | collective-permute-done | bytes 1048608 | tf_op jit(solution)/shard_map/ppermute | solution.py:19
  198.3 6.0 %broadcast_in_dim.2 = bf16[2048,4096]{1,0:T(8,128)(2,1)} broadcast(bf16[]{:T(256)} %constant.137.clone.1), dimensions={} | broadcast | bytes 16777218 | tf_op jit(solution)/shard_map/broadcast_in_dim | solution.py:13
  205.3 2.5 collective-permute-done.10
  211.8 11.5 %collective-permute-done.11 = bf16[128,4096]{1,0:T(8,128)(2,1)} collective-permute-done((bf16[128,4096]{1,0:T(8,128)(2,1)}, bf16[128,4096]{1,0:T(8,128)(2,1)}, u32[]{:S(2)}, u32[]{:S(2)}) %collective-permute-start.11) | collective-permute-done | bytes 1048608 | tf_op jit(solution)/shard_map/ppermute | solution.py:19
  224.3 2.9 copy.23
  227.2 2.3 constant_dynamic-update-slice_fusion.11
  229.5 2.3 constant_dynamic-update-slice_fusion.10
  231.9 6.8 %collective-permute-done.12 = bf16[128,4096]{1,0:T(8,128)(2,1)} collective-permute-done((bf16[128,4096]{1,0:T(8,128)(2,1)}, bf16[128,4096]{1,0:T(8,128)(2,1)}, u32[]{:S(2)}, u32[]{:S(2)}) %collective-permute-start.12) | collective-permute-done | bytes 1048608 | tf_op jit(solution)/shard_map/ppermute | solution.py:19
  238.7 2.4 constant_dynamic-update-slice_fusion.9
  241.1 2.3 constant_dynamic-update-slice_fusion.8
  243.4 2.3 constant_dynamic-update-slice_fusion.7
  245.7 8.3 %collective-permute-done.13 = bf16[128,4096]{1,0:T(8,128)(2,1)S(1)} collective-permute-done((bf16[128,4096]{1,0:T(8,128)(2,1)}, bf16[128,4096]{1,0:T(8,128)(2,1)S(1)}, u32[]{:S(2)}, u32[]{:S(2)}) %collective-permute-start.13) | collective-permute-done | bytes 1048608 | tf_op jit(solution)/shard_map/ppermute | solution.py:19
  255.1 2.3 constant_dynamic-update-slice_fusion.5
  257.4 2.3 constant_dynamic-update-slice_fusion.4
  259.7 9.4 %collective-permute-done.14 = bf16[128,4096]{1,0:T(8,128)(2,1)S(1)} collective-permute-done((bf16[128,4096]{1,0:T(8,128)(2,1)S(1)}, bf16[128,4096]{1,0:T(8,128)(2,1)S(1)}, u32[]{:S(2)}, u32[]{:S(2)}) %collective-permute-start.14) | collective-permute-done | bytes 1048608 | tf_op jit(solution)/shard_map/ppermute | solution.py:19
  269.1 2.3 constant_dynamic-update-slice_fusion.3
  273.5 10.8 %collective-permute-done.15 = bf16[128,4096]{1,0:T(8,128)(2,1)S(1)} collective-permute-done((bf16[128,4096]{1,0:T(8,128)(2,1)S(1)}, bf16[128,4096]{1,0:T(8,128)(2,1)S(1)}, u32[]{:S(2)}, u32[]{:S(2)}) %collective-permute-start.15) | collective-permute-done | bytes 1048608 | tf_op jit(solution)/shard_map/ppermute | solution.py:19
  285.4 8.3 %convolution_bitcast_fusion = f32[256,2048]{1,0:T(8,128)S(1)} fusion(bf16[2048,4096]{1,0:T(8,128)(2,1)} %constant_dynamic-update-slice_fusion, bf16[256,4096]{1,0:T(8,128)(2,1)S(1)} %copy-done), kind=kOutput, calls=%fused_computation.7 | convolution fusion | flops 4294967296 | bytes 20971520 | tf_op jit(solution)/shard_map/dot_general | solution.py:152
  293.7 2.2 multiply_bitcast_fusion
  297.5 7.4 %all-to-all-start.2 = ((f32[16,128,256]{1,2,0:T(8,128)}), f32[16,128,256]{1,2,0:T(8,128)}, u32[]{:S(2)}, u32[]{:S(2)}) async-start(f32[16,128,256]{1,2,0:T(8,128)} %bitcast.123), calls=%async_computation.2 | async-start | bytes 4194304 | tf_op jit(solution)/shard_map/all_to_all | solution.py:72
  304.9 2.8 fusion.4
  307.8 2.0 copy-done.5
  311.1 41.5 %all-to-all-done.2 = f32[16,128,256]{1,2,0:T(8,128)} async-done(((f32[16,128,256]{1,2,0:T(8,128)}), f32[16,128,256]{1,2,0:T(8,128)}, u32[]{:S(2)}, u32[]{:S(2)}) %all-to-all-start.2) | async-done | bytes 2097184 | tf_op jit(solution)/shard_map/all_to_all | solution.py:72
  352.6 16.5 %rev.11 = f32[128,32,128]{0,2,1:T(8,128)} reverse(f32[128,32,128]{0,2,1:T(8,128)} %bitcast.33), dimensions={1,2} | reverse | bytes 4194304 | tf_op jit(solution)/shard_map/jit(_flip)/rev | solution.py:83
  369.2 1.9 copy.27
  371.1 2.8 fusion.7
  374.0 1.9 copy-done.6
  377.3 6.8 %multiply_reduce_fusion = (f32[128,32,128]{0,2,1:T(8,128)S(1)}, f32[128,32,128]{0,2,1:T(8,128)}) fusion(f32[2,128,32,128]{1,3,2,0:T(8,128)} %copy-done.6, f32[2,128,32]{1,2,0:T(8,128)S(1)} %pad_multiply_fusion, f32[2,128]{1,0:T(2,128)S(1)} %copy-done.42, f32[2,128,128]{1,2,0:T(8,128)S(1)} %get-tuple-element.90, f32[2,128,32,128]{1,3,2,0:T(8,128)} %copy-done.5, ...), kind=kLoop, calls=%fused_computation.1 | loop fusion | flops 7340032 | bytes 12780544 | tf_op jit(solution)/shard_map/reduce_sum | solution.py:67
  384.0 4.7 all-to-all-start.1
  388.7 10.1 %rev.13 = f32[128,32,128]{0,2,1:T(8,128)} reverse(f32[128,32,128]{0,2,1:T(8,128)S(1)} %get-tuple-element.4), dimensions={1,2} | reverse | bytes 4194304 | tf_op jit(solution)/shard_map/jit(_flip)/rev | solution.py:91
  398.9 37.6 %all-to-all-done.1 = f32[128,16,256]{0,2,1:T(8,128)} async-done(((f32[128,16,256]{0,2,1:T(8,128)}), f32[128,16,256]{0,2,1:T(8,128)}, u32[]{:S(2)}, u32[]{:S(2)}) %all-to-all-start.1) | async-done | bytes 2097184 | tf_op jit(solution)/shard_map/all_to_all | solution.py:92
  436.5 4.8 all-to-all-start.3
  441.4 47.7 %all-to-all-done.3 = f32[128,16,256]{0,2,1:T(8,128)} async-done(((f32[128,16,256]{0,2,1:T(8,128)}), f32[128,16,256]{0,2,1:T(8,128)}, u32[]{:S(2)}, u32[]{:S(2)}) %all-to-all-start.3) | async-done | bytes 2097184 | tf_op jit(solution)/shard_map/all_to_all | solution.py:92
  489.0 5.2 %fusion.65 = (f32[256,2048]{1,0:T(8,128)S(1)}, f32[256,2048]{1,0:T(8,128)S(1)}, f32[256,2048]{1,0:T(8,128)S(1)}, f32[256,2048]{1,0:T(8,128)S(1)}) fusion(f32[256,2048]{1,0:T(8,128)} %get-tuple-element.13, f32[256,2048]{1,0:T(8,128)} %copy-done.8, f32[256,2048]{1,0:T(8,128)} %get-tuple-element.18, f32[2048]{0:T(1024)S(1)} %copy-done.40, ...), kind=kLoop, calls=%fused_computation.207 | loop fusion | flops 4194304 | bytes 20979712 | tf_op jit(solution)/shard_map/mul | solution.py:163
  494.7 3.2 collective-permute-start.16
  497.9 11.6 %convolution_convert_fusion = bf16[256,4096]{1,0:T(8,128)(2,1)} fusion(bf16[2048,4096]{1,0:T(8,128)(2,1)} %constant_dynamic-update-slice_fusion, f32[256,2048]{1,0:T(8,128)S(1)} %copy-done.7, f32[256,2048]{1,0:T(8,128)S(1)} %get-tuple-element.20), kind=kOutput, calls=%fused_computation | convolution fusion | flops 4297064448 | bytes 23068672 | tf_op jit(solution)/shard_map/dot_general | solution.py:151
  509.6 1.9 fusion.24
  511.5 4.2 fusion.14
  (309 shorter events, 36.0 us)
Async XLA Ops:
  0.6 284.7 %copy-start = (bf16[256,4096]{1,0:T(8,128)(2,1)S(1)}, bf16[256,4096]{1,0:T(8,128)(2,1)}, u32[]{:S(2)}) copy-start(bf16[256,4096]{1,0:T(8,128)(2,1)} %param.18) | copy-start | bytes 6291460
  0.6 109.7 %copy-start.9 = (bf16[256,2048]{1,0:T(8,128)(2,1)S(1)}, bf16[256,2048]{1,0:T(8,128)(2,1)}, u32[]{:S(2)}) copy-start(bf16[256,2048]{1,0:T(8,128)(2,1)} %param.11) | copy-start | bytes 3145732
  0.7 15.4 %collective-permute-start.1 = (bf16[128,4096]{1,0:T(8,128)(2,1)}, bf16[128,4096]{1,0:T(8,128)(2,1)S(1)}, u32[]{:S(2)}, u32[]{:S(2)}) collective-permute-start(bf16[128,4096]{1,0:T(8,128)(2,1)} %param.17), channel_id=1, source_target_pairs={{0,1},{1,2},{2,3},{3,4},{4,5},{5,6},{6,7},{7,8},{8,9},{9,10},{10,1... | collective-permute-start | bytes 3145736 | tf_op jit(solution)/shard_map/ppermute | solution.py:19
  16.0 15.1 %collective-permute-start.2 = (bf16[128,4096]{1,0:T(8,128)(2,1)S(1)}, bf16[128,4096]{1,0:T(8,128)(2,1)S(1)}, u32[]{:S(2)}, u32[]{:S(2)}) collective-permute-start(bf16[128,4096]{1,0:T(8,128)(2,1)S(1)} %collective-permute-done.1), channel_id=1, source_target_pairs={{0,1},{1,2},{2,3},{3,4},{4,5},{5,6},{6,7},{7,8},{8,9},{9,10},{10,1... | collective-permute-start | bytes 3145736 | tf_op jit(solution)/shard_map/ppermute | solution.py:19
  31.2 31.3 %copy-start.16 = (bf16[128,4096]{1,0:T(8,128)(2,1)}, bf16[128,4096]{1,0:T(8,128)(2,1)S(1)}, u32[]{:S(2)}) copy-start(bf16[128,4096]{1,0:T(8,128)(2,1)S(1)} %collective-permute-done.2) | copy-start | bytes 3145732
  31.2 15.1 %collective-permute-start.3 = (bf16[128,4096]{1,0:T(8,128)(2,1)S(1)}, bf16[128,4096]{1,0:T(8,128)(2,1)S(1)}, u32[]{:S(2)}, u32[]{:S(2)}) collective-permute-start(bf16[128,4096]{1,0:T(8,128)(2,1)S(1)} %collective-permute-done.2), channel_id=1, source_target_pairs={{0,1},{1,2},{2,3},{3,4},{4,5},{5,6},{6,7},{7,8},{8,9},{9,10},{10,1... | collective-permute-start | bytes 3145736 | tf_op jit(solution)/shard_map/ppermute | solution.py:19
  47.3 15.2 %collective-permute-start.4 = (bf16[128,4096]{1,0:T(8,128)(2,1)S(1)}, bf16[128,4096]{1,0:T(8,128)(2,1)}, u32[]{:S(2)}, u32[]{:S(2)}) collective-permute-start(bf16[128,4096]{1,0:T(8,128)(2,1)S(1)} %collective-permute-done.3), channel_id=1, source_target_pairs={{0,1},{1,2},{2,3},{3,4},{4,5},{5,6},{6,7},{7,8},{8,9},{9,10},{10,1... | collective-permute-start | bytes 3145736 | tf_op jit(solution)/shard_map/ppermute | solution.py:19
  62.5 15.4 %collective-permute-start.5 = (bf16[128,4096]{1,0:T(8,128)(2,1)}, bf16[128,4096]{1,0:T(8,128)(2,1)}, u32[]{:S(2)}, u32[]{:S(2)}) collective-permute-start(bf16[128,4096]{1,0:T(8,128)(2,1)} %collective-permute-done.4), channel_id=1, source_target_pairs={{0,1},{1,2},{2,3},{3,4},{4,5},{5,6},{6,7},{7,8},{8,9},{9,10},{10,1... | collective-permute-start | bytes 3145736 | tf_op jit(solution)/shard_map/ppermute | solution.py:19
  64.1 31.7 %collective-permute-start = (bf16[3,2,2048]{2,1,0:T(2,128)(2,1)S(1)}, bf16[3,2,2048]{2,1,0:T(2,128)(2,1)S(1)}, u32[]{:S(2)}, u32[]{:S(2)}) collective-permute-start(bf16[3,2,2048]{2,1,0:T(2,128)(2,1)S(1)} %pad_maximum_fusion.3), channel_id=1, source_target_pairs={{0,1},{1,2},{2,3},{3,4},{4,5},{5,6},{6,7},{7,8},{8,9},{9,10},{10,1... | collective-permute-start | bytes 73736 | tf_op jit(solution)/shard_map/ppermute | solution.py:26
  77.9 15.4 %collective-permute-start.6 = (bf16[128,4096]{1,0:T(8,128)(2,1)}, bf16[128,4096]{1,0:T(8,128)(2,1)}, u32[]{:S(2)}, u32[]{:S(2)}) collective-permute-start(bf16[128,4096]{1,0:T(8,128)(2,1)} %collective-permute-done.5), channel_id=1, source_target_pairs={{0,1},{1,2},{2,3},{3,4},{4,5},{5,6},{6,7},{7,8},{8,9},{9,10},{10,1... | collective-permute-start | bytes 3145736 | tf_op jit(solution)/shard_map/ppermute | solution.py:19
  93.4 15.4 %collective-permute-start.7 = (bf16[128,4096]{1,0:T(8,128)(2,1)}, bf16[128,4096]{1,0:T(8,128)(2,1)}, u32[]{:S(2)}, u32[]{:S(2)}) collective-permute-start(bf16[128,4096]{1,0:T(8,128)(2,1)} %collective-permute-done.6), channel_id=1, source_target_pairs={{0,1},{1,2},{2,3},{3,4},{4,5},{5,6},{6,7},{7,8},{8,9},{9,10},{10,1... | collective-permute-start | bytes 3145736 | tf_op jit(solution)/shard_map/ppermute | solution.py:19
  93.5 17.2 %copy-start.36 = (f32[256]{0:T(256)}, f32[256]{0:T(256)S(1)}, u32[]{:S(2)}) copy-start(f32[256]{0:T(256)S(1)} %get-tuple-element.84) | copy-start | bytes 3076
  93.5 17.2 %copy-start.38 = (f32[256]{0:T(256)}, f32[256]{0:T(256)S(1)}, u32[]{:S(2)}) copy-start(f32[256]{0:T(256)S(1)} %get-tuple-element.85) | copy-start | bytes 3076
  95.1 15.6 %copy-start.18 = (f32[1,1,2048]{2,1,0:T(1,128)}, f32[1,1,2048]{2,1,0:T(1,128)S(1)}, u32[]{:S(2)}) copy-start(f32[1,1,2048]{2,1,0:T(1,128)S(1)} %get-tuple-element.23) | copy-start | bytes 24580
  95.1 15.6 %copy-start.20 = (f32[1,1,2048]{2,1,0:T(1,128)}, f32[1,1,2048]{2,1,0:T(1,128)S(1)}, u32[]{:S(2)}) copy-start(f32[1,1,2048]{2,1,0:T(1,128)S(1)} %get-tuple-element.24) | copy-start | bytes 24580
  95.1 15.6 %copy-start.22 = (f32[1,1,2048]{2,1,0:T(1,128)}, f32[1,1,2048]{2,1,0:T(1,128)S(1)}, u32[]{:S(2)}) copy-start(f32[1,1,2048]{2,1,0:T(1,128)S(1)} %get-tuple-element.28) | copy-start | bytes 24580
  95.1 15.6 %copy-start.24 = (f32[1,1,2048]{2,1,0:T(1,128)}, f32[1,1,2048]{2,1,0:T(1,128)S(1)}, u32[]{:S(2)}) copy-start(f32[1,1,2048]{2,1,0:T(1,128)S(1)} %get-tuple-element.29) | copy-start | bytes 24580
  108.8 24.8 %collective-permute-start.8 = (bf16[128,4096]{1,0:T(8,128)(2,1)}, bf16[128,4096]{1,0:T(8,128)(2,1)}, u32[]{:S(2)}, u32[]{:S(2)}) collective-permute-start(bf16[128,4096]{1,0:T(8,128)(2,1)} %collective-permute-done.7), channel_id=1, source_target_pairs={{0,1},{1,2},{2,3},{3,4},{4,5},{5,6},{6,7},{7,8},{8,9},{9,10},{10,1... | collective-permute-start | bytes 3145736 | tf_op jit(solution)/shard_map/ppermute | solution.py:19
  115.5 108.8 %all-to-all-start = ((f32[16,128,256]{1,2,0:T(8,128)}), f32[16,128,256]{1,2,0:T(8,128)}, u32[]{:S(2)}, u32[]{:S(2)}) async-start(f32[16,128,256]{1,2,0:T(8,128)} %bitcast.122), calls=%async_computation | async-start | bytes 4194304 | tf_op jit(solution)/shard_map/all_to_all | solution.py:72
  133.7 58.9 %collective-permute-start.9 = (bf16[128,4096]{1,0:T(8,128)(2,1)}, bf16[128,4096]{1,0:T(8,128)(2,1)S(1)}, u32[]{:S(2)}, u32[]{:S(2)}) collective-permute-start(bf16[128,4096]{1,0:T(8,128)(2,1)} %collective-permute-done.8), channel_id=1, source_target_pairs={{0,1},{1,2},{2,3},{3,4},{4,5},{5,6},{6,7},{7,8},{8,9},{9,10},{10,1... | collective-permute-start | bytes 3145736 | tf_op jit(solution)/shard_map/ppermute | solution.py:19
  135.6 61.8 %copy-start.47 = (f32[32]{0:T(128)}, f32[32]{0:T(128)S(1)}, u32[]{:S(2)}) copy-start(f32[32]{0:T(128)S(1)} %convert_subtract_fusion) | copy-start | bytes 388
  135.6 61.8 %copy-start.45 = (f32[32]{0:T(128)}, f32[32]{0:T(128)S(1)}, u32[]{:S(2)}) copy-start(f32[32]{0:T(128)S(1)} %broadcast_subtract_fusion.1) | copy-start | bytes 388
  192.6 15.2 %collective-permute-start.10 = (bf16[128,4096]{1,0:T(8,128)(2,1)S(1)}, bf16[128,4096]{1,0:T(8,128)(2,1)}, u32[]{:S(2)}, u32[]{:S(2)}) collective-permute-start(bf16[128,4096]{1,0:T(8,128)(2,1)S(1)} %collective-permute-done.9), channel_id=1, source_target_pairs={{0,1},{1,2},{2,3},{3,4},{4,5},{5,6},{6,7},{7,8},{8,9},{9,10},{10,1... | collective-permute-start | bytes 3145736 | tf_op jit(solution)/shard_map/ppermute | solution.py:19
  198.2 6.0 %copy-start.11 = (bf16[128,4096]{1,0:T(8,128)(2,1)S(1)}, bf16[128,4096]{1,0:T(8,128)(2,1)}, u32[]{:S(2)}) copy-start(bf16[128,4096]{1,0:T(8,128)(2,1)} %param.17) | copy-start | bytes 3145732
  207.8 15.4 %collective-permute-start.11 = (bf16[128,4096]{1,0:T(8,128)(2,1)}, bf16[128,4096]{1,0:T(8,128)(2,1)}, u32[]{:S(2)}, u32[]{:S(2)}) collective-permute-start(bf16[128,4096]{1,0:T(8,128)(2,1)} %collective-permute-done.10), channel_id=1, source_target_pairs={{0,1},{1,2},{2,3},{3,4},{4,5},{5,6},{6,7},{7,8},{8,9},{9,10},{10,1... | collective-permute-start | bytes 3145736 | tf_op jit(solution)/shard_map/ppermute | solution.py:19
  209.6 13.7 %copy-start.13 = (bf16[128,4096]{1,0:T(8,128)(2,1)S(1)}, bf16[128,4096]{1,0:T(8,128)(2,1)}, u32[]{:S(2)}) copy-start(bf16[128,4096]{1,0:T(8,128)(2,1)} %copy-done.12) | copy-start | bytes 3145732
  223.2 15.4 %collective-permute-start.12 = (bf16[128,4096]{1,0:T(8,128)(2,1)}, bf16[128,4096]{1,0:T(8,128)(2,1)}, u32[]{:S(2)}, u32[]{:S(2)}) collective-permute-start(bf16[128,4096]{1,0:T(8,128)(2,1)} %collective-permute-done.11), channel_id=1, source_target_pairs={{0,1},{1,2},{2,3},{3,4},{4,5},{5,6},{6,7},{7,8},{8,9},{9,10},{10,1... | collective-permute-start | bytes 3145736 | tf_op jit(solution)/shard_map/ppermute | solution.py:19
  238.7 15.3 %collective-permute-start.13 = (bf16[128,4096]{1,0:T(8,128)(2,1)}, bf16[128,4096]{1,0:T(8,128)(2,1)S(1)}, u32[]{:S(2)}, u32[]{:S(2)}) collective-permute-start(bf16[128,4096]{1,0:T(8,128)(2,1)} %collective-permute-done.12), channel_id=1, source_target_pairs={{0,1},{1,2},{2,3},{3,4},{4,5},{5,6},{6,7},{7,8},{8,9},{9,10},{10,1... | collective-permute-start | bytes 3145736 | tf_op jit(solution)/shard_map/ppermute | solution.py:19
  254.0 15.1 %collective-permute-start.14 = (bf16[128,4096]{1,0:T(8,128)(2,1)S(1)}, bf16[128,4096]{1,0:T(8,128)(2,1)S(1)}, u32[]{:S(2)}, u32[]{:S(2)}) collective-permute-start(bf16[128,4096]{1,0:T(8,128)(2,1)S(1)} %collective-permute-done.13), channel_id=1, source_target_pairs={{0,1},{1,2},{2,3},{3,4},{4,5},{5,6},{6,7},{7,8},{8,9},{9,10},{10,1... | collective-permute-start | bytes 3145736 | tf_op jit(solution)/shard_map/ppermute | solution.py:19
  269.1 15.1 %collective-permute-start.15 = (bf16[128,4096]{1,0:T(8,128)(2,1)S(1)}, bf16[128,4096]{1,0:T(8,128)(2,1)S(1)}, u32[]{:S(2)}, u32[]{:S(2)}) collective-permute-start(bf16[128,4096]{1,0:T(8,128)(2,1)S(1)} %collective-permute-done.14), channel_id=1, source_target_pairs={{0,1},{1,2},{2,3},{3,4},{4,5},{5,6},{6,7},{7,8},{8,9},{9,10},{10,1... | collective-permute-start | bytes 3145736 | tf_op jit(solution)/shard_map/ppermute | solution.py:19
  285.3 8.4 %copy-start.2 = (f32[258,2048]{1,0:T(8,128)S(1)}, f32[258,2048]{1,0:T(8,128)}, u32[]{:S(2)}) copy-start(f32[258,2048]{1,0:T(8,128)} %maximum_convert_fusion) | copy-start | bytes 6340612
  285.3 8.4 %copy-start.26 = (f32[1,1,2048]{2,1,0:T(1,128)S(1)}, f32[1,1,2048]{2,1,0:T(1,128)}, u32[]{:S(2)}) copy-start(f32[1,1,2048]{2,1,0:T(1,128)} %get-tuple-element.25) | copy-start | bytes 24580
  285.3 8.4 %copy-start.27 = (f32[1,1,2048]{2,1,0:T(1,128)S(1)}, f32[1,1,2048]{2,1,0:T(1,128)}, u32[]{:S(2)}) copy-start(f32[1,1,2048]{2,1,0:T(1,128)} %get-tuple-element.26) | copy-start | bytes 24580
  285.3 8.4 %copy-start.28 = (f32[1,1,2048]{2,1,0:T(1,128)S(1)}, f32[1,1,2048]{2,1,0:T(1,128)}, u32[]{:S(2)}) copy-start(f32[1,1,2048]{2,1,0:T(1,128)} %get-tuple-element.27) | copy-start | bytes 24580
  285.3 8.4 %copy-start.37 = (f32[256]{0:T(256)S(1)}, f32[256]{0:T(256)}, u32[]{:S(2)}) copy-start(f32[256]{0:T(256)} %copy-done.36) | copy-start | bytes 3076
  285.4 8.4 %copy-start.39 = (f32[256]{0:T(256)S(1)}, f32[256]{0:T(256)}, u32[]{:S(2)}) copy-start(f32[256]{0:T(256)} %copy-done.38) | copy-start | bytes 3076
  297.5 7.4 %copy-start.3 = (f32[128,32,128]{2,0,1:T(8,128)S(1)}, f32[128,32,128]{2,0,1:T(8,128)}, u32[]{:S(2)}) copy-start(f32[128,32,128]{2,0,1:T(8,128)} %copy.23) | copy-start | bytes 6291460
  297.5 55.1 %all-to-all-start.2 = ((f32[16,128,256]{1,2,0:T(8,128)}), f32[16,128,256]{1,2,0:T(8,128)}, u32[]{:S(2)}, u32[]{:S(2)}) async-start(f32[16,128,256]{1,2,0:T(8,128)} %bitcast.123), calls=%async_computation.2 | async-start | bytes 4194304 | tf_op jit(solution)/shard_map/all_to_all | solution.py:72
  304.9 6.0 %copy-start.44 = (f32[2,128,1]{1,2,0:T(1,128)S(1)}, f32[2,128,1]{1,2,0:T(1,128)}, u32[]{:S(2)}) copy-start(f32[2,128,1]{1,2,0:T(1,128)} %slice.607) | copy-start | bytes 3076
  304.9 6.1 %copy-start.48 = (f32[32]{0:T(128)S(1)}, f32[32]{0:T(128)}, u32[]{:S(2)}) copy-start(f32[32]{0:T(128)} %copy-done.47) | copy-start | bytes 388
  371.1 5.9 %copy-start.43 = (f32[2,128,1]{1,2,0:T(1,128)S(1)}, f32[2,128,1]{1,2,0:T(1,128)}, u32[]{:S(2)}) copy-start(f32[2,128,1]{1,2,0:T(1,128)} %slice.639) | copy-start | bytes 3076
  371.1 6.1 %copy-start.46 = (f32[32]{0:T(128)S(1)}, f32[32]{0:T(128)}, u32[]{:S(2)}) copy-start(f32[32]{0:T(128)} %copy-done.45) | copy-start | bytes 388
  371.1 6.1 %copy-start.42 = (f32[2,128]{1,0:T(2,128)S(1)}, f32[2,128]{1,0:T(2,128)}, u32[]{:S(2)}) copy-start(f32[2,128]{1,0:T(2,128)} %get-tuple-element.15) | copy-start | bytes 3076
  384.0 52.4 %all-to-all-start.1 = ((f32[128,16,256]{0,2,1:T(8,128)}), f32[128,16,256]{0,2,1:T(8,128)}, u32[]{:S(2)}, u32[]{:S(2)}) async-start(f32[128,16,256]{0,2,1:T(8,128)} %bitcast.121), calls=%async_computation.1 | async-start | bytes 4194304 | tf_op jit(solution)/shard_map/all_to_all | solution.py:92
  436.5 52.6 %copy-start.4 = (f32[256,2048]{1,0:T(8,128)S(1)}, f32[256,2048]{1,0:T(8,128)}, u32[]{:S(2)}) copy-start(f32[256,2048]{1,0:T(8,128)} %get-tuple-element.14) | copy-start | bytes 6291460
  436.5 52.6 %copy-start.40 = (f32[2048]{0:T(1024)S(1)}, f32[2048]{0:T(1024)}, u32[]{:S(2)}) copy-start(f32[2048]{0:T(1024)} %param.16) | copy-start | bytes 24580
  436.5 52.6 %all-to-all-start.3 = ((f32[128,16,256]{0,2,1:T(8,128)}), f32[128,16,256]{0,2,1:T(8,128)}, u32[]{:S(2)}, u32[]{:S(2)}) async-start(f32[128,16,256]{0,2,1:T(8,128)} %bitcast.124), calls=%async_computation.3 | async-start | bytes 4194304 | tf_op jit(solution)/shard_map/all_to_all | solution.py:92
  494.7 14.8 %collective-permute-start.16 = (bf16[3,2,2048]{2,1,0:T(2,128)(2,1)S(1)}, bf16[3,2,2048]{2,1,0:T(2,128)(2,1)S(1)}, u32[]{:S(2)}, u32[]{:S(2)}) collective-permute-start(bf16[3,2,2048]{2,1,0:T(2,128)(2,1)S(1)} %pad_maximum_fusion.4), channel_id=1, source_target_pairs={{1,0},{2,1},{3,2},{4,3},{5,4},{6,5},{7,6},{8,7},{9,8},{10,9},{11,1... | collective-permute-start | bytes 73736 | tf_op jit(solution)/shard_map/ppermute | solution.py:26
  (22 other events, 74.3 us)
